TPU v7x, 256 devices: a whole 4x4x8 slice. The times are simulated.
256 devices in a mesh: op: 64 (over z, x, core), sec: 4 (over y).
Axes of the slice: x: 4, y: 4, z: 8, core: 2. Of those that a mesh axis runs over, the one named last changes fastest.
Arguments:
- wavefunction: bfloat16 [40, 128, 128], P('sec'), may hold values from -6 to 6
- diagonal: float32 [40, 128, 128], P('sec'), may hold values from -2 to 2
- left_ops: bfloat16 [1024, 40, 128, 128], P('op', 'sec'), may hold values from -0.15 to 0.2171875
- right_ops: bfloat16 [1024, 40, 128, 128], P('op', 'sec'), may hold values from -0.6 to 1.6
- connect: int32 [1024, 40], P('op', 'sec'), may hold values from 0 to 40, as said below
Outputs:
- sigma_one: bfloat16 [40, 128, 128], P('sec')
- correction: bfloat16 [40, 128, 128], P('sec')
- sigma_two: bfloat16 [40, 128, 128], P('sec')
Inputs may be any that keep to these rules, and one draw needn't show every extreme that they name: connect[p,b] is (b + s_p) mod 40 for a shift s_p of pair p, or 40 where pair p does not act into sector b.
All inputs are finite; a program needn't handle non-finite values.
Results may differ from a plain program's by a relative error of at most 0.005.
Values may be sent and summed in bfloat16 or wider, within the bound.
A program may use at most 128 MiB of HBM per device.

v0:
```python
import jax
import jax.numpy as jnp
from jax import lax
from jax.sharding import PartitionSpec as P


def build_terms(vector, left_ops, right_ops, connect):
    gathered = lax.all_gather(vector, "sec", axis=0, tiled=True)
    block_len = gathered.shape[1]
    padded = jnp.concatenate(
        [gathered, jnp.zeros((1, block_len, block_len), gathered.dtype)], axis=0
    )
    pair_dev, sec_dev = connect.shape
    sources = jnp.take(padded, connect.reshape(-1), axis=0)
    left_flat = left_ops.reshape(pair_dev * sec_dev, block_len, block_len)
    right_flat = right_ops.reshape(pair_dev * sec_dev, block_len, block_len)
    halfway = jnp.einsum(
        "nij,njk->nik", left_flat, sources, preferred_element_type=jnp.float32
    ).astype(jnp.bfloat16)
    products = jnp.einsum("nik,nlk->nil", halfway, right_flat, preferred_element_type=jnp.float32)
    return jnp.sum(products.reshape(pair_dev, sec_dev, block_len, block_len), axis=0)


def refine(psi_part, diag_part, sigma_part, first_sums, second_sums, total_cells):
    psi_wide = psi_part.astype(jnp.float32)
    correlation, weight = first_sums((jnp.sum(psi_wide * sigma_part), jnp.sum(psi_wide * psi_wide)))
    rayleigh = correlation / weight
    shifted = diag_part - rayleigh
    unscaled = (sigma_part - rayleigh * psi_wide) * shifted / (shifted * shifted + 1.0)
    along, squares = second_sums((jnp.sum(psi_wide * unscaled), jnp.sum(unscaled * unscaled)))
    rescale = 1.0 / jnp.sqrt((squares - along * along / weight) / total_cells + 1e-06)
    return ((unscaled - along / weight * psi_wide) * rescale).astype(jnp.bfloat16)


def per_device(wavefunction, diagonal, left_ops, right_ops, connect):
    total_cells = float(
        lax.axis_size("sec") * wavefunction.shape[0] * wavefunction.shape[1] * wavefunction.shape[2]
    )
    partial_value = build_terms(wavefunction, left_ops, right_ops, connect)

    def whole_sum(summands):
        return lax.psum(summands, "op")

    def first_whole(summands):
        return lax.psum(summands, "sec")

    def second_whole(summands):
        return lax.psum(summands, "sec")

    sigma = whole_sum(partial_value)
    correction = refine(wavefunction, diagonal, sigma, first_whole, second_whole, total_cells)
    sigma_two = whole_sum(build_terms(correction, left_ops, right_ops, connect))
    return (sigma.astype(jnp.bfloat16), correction, sigma_two.astype(jnp.bfloat16))


def solution(mesh):
    placed = (
        P("sec", None, None),
        P("sec", None, None),
        P("op", "sec", None, None),
        P("op", "sec", None, None),
        P("op", "sec"),
    )
    return jax.shard_map(
        per_device,
        mesh=mesh,
        in_specs=placed,
        out_specs=(P("sec", None, None), P("sec", None, None), P("sec", None, None)),
        check_vma=False,
    )
```

profile of v0, /device:TPU:1, one launch (start us, length us, event | category | flops | bytes accessed | tf_op | source)
XLA Modules:
  0.0 594.7 jit_solution(585796697513924323)
XLA Ops:
  7.2 0.0 all-gather.3.cloned.1.call-start
  7.2 0.7 all-gather.3.cloned.1.call-update
  7.9 0.0 all-reduce.7.cloned.1.call-start
  7.9 0.8 reshape.29
  8.8 31.2 %all-gather.3.cloned.1.call-done = bf16[40,128,128]{2,1,0:T(8,128)(2,1)} async-done(((bf16[10,128,128]{2,1,0:T(8,128)(2,1)}), bf16[40,128,128]{2,1,0:T(8,128)(2,1)}) %all-gather.3.cloned.1.call-update) | async-done | bytes 1310736 | tf_op jit(solution)/shard_map/all_gather | solution.py:8
  39.9 1.4 concatenate.6
  41.4 7.7 %gather_fusion = bf16[160,128,128]{2,1,0:T(8,128)(2,1)} fusion(bf16[41,128,128]{2,1,0:T(8,128)(2,1)S(1)} %concatenate.6, s32[1024]{0:T(1024)S(1)} %pad_clamp_fusion), kind=kCustom, calls=%fused_computation.clone | custom fusion | bytes 10486400 | tf_op jit(solution)/shard_map/jit(_take)/gather | solution.py:14
  49.0 14.8 %fusion.6 = f32[160,128,128]{2,1,0:T(8,128)} fusion(bf16[160,128,128]{2,1,0:T(8,128)(2,1)} %bitcast.10, bf16[160,128,128]{2,1,0:T(8,128)(2,1)} %bitcast.12, bf16[160,128,128]{2,1,0:T(8,128)(2,1)} %gather_fusion, pred[160]{0:T(512)(128)(4,1)S(1)} %compare_and_fusion), kind=kOutput, calls=%fused_computation.8 | convolution fusion | flops 1347420160 | bytes 26214560 | tf_op jit(solution)/shard_map/nik,nlk->nil/dot_general | solution.py:20
  63.8 0.0 copy-start
  63.8 0.0 copy-start.1
  63.8 5.7 reduce_sum.54
  69.6 0.0 all-reduce.7.cloned.1.call-update
  69.6 0.0 all-gather.5.cloned.1.call-start
  69.6 182.7 %all-reduce.7.cloned.1.call-done = f32[10,128,128]{2,1,0:T(8,128)} async-done(((f32[10,128,128]{2,1,0:T(8,128)}), f32[10,128,128]{2,1,0:T(8,128)}) %all-reduce.7.cloned.1.call-update) | async-done | bytes 655376 | tf_op jit(solution)/shard_map/psum | solution.py:42
  252.3 0.0 copy-done
  252.3 1.9 fusion.23
  254.2 9.1 %all-reduce.3 = (f32[]{:T(128)}, f32[]{:T(128)}) all-reduce(f32[]{:T(128)} %get-tuple-element.7, f32[]{:T(128)} %get-tuple-element.6), channel_id=1, replica_groups=mesh['op'=64,'sec'=4] {'sec'}, use_global_device_ids=true, to_apply=%region_3.5 | all-reduce | flops 2 | bytes 16 | tf_op jit(solution)/shard_map/psum | solution.py:45
  264.6 0.0 copy-done.1
  264.6 2.9 fusion.27
  267.5 6.9 %all-reduce.2 = (f32[]{:T(128)}, f32[]{:T(128)}) all-reduce(f32[]{:T(128)} %get-tuple-element.5, f32[]{:T(128)} %get-tuple-element.4), channel_id=1, replica_groups=mesh['op'=64,'sec'=4] {'sec'}, use_global_device_ids=true, to_apply=%region_9.11 | all-reduce | flops 2 | bytes 16 | tf_op jit(solution)/shard_map/psum | solution.py:48
  278.4 0.8 fusion.30
  279.3 0.0 all-gather.5.cloned.1.call-update
  279.3 27.8 %all-gather.5.cloned.1.call-done = bf16[40,128,128]{2,1,0:T(8,128)(2,1)} async-done(((bf16[10,128,128]{2,1,0:T(8,128)(2,1)}), bf16[40,128,128]{2,1,0:T(8,128)(2,1)}) %all-gather.5.cloned.1.call-update) | async-done | bytes 1310736 | tf_op jit(solution)/shard_map/all_gather | solution.py:8
  307.1 1.4 concatenate.7
  308.5 7.7 %gather_fusion.1 = bf16[160,128,128]{2,1,0:T(8,128)(2,1)} fusion(bf16[41,128,128]{2,1,0:T(8,128)(2,1)S(1)} %concatenate.7, s32[1024]{0:T(1024)S(1)} %pad_clamp_fusion), kind=kCustom, calls=%fused_computation.1.clone | custom fusion | bytes 10486400 | tf_op jit(solution)/shard_map/jit(_take)/gather | solution.py:14
  316.2 14.8 %fusion.4 = f32[160,128,128]{2,1,0:T(8,128)} fusion(bf16[160,128,128]{2,1,0:T(8,128)(2,1)} %bitcast.11, bf16[160,128,128]{2,1,0:T(8,128)(2,1)} %bitcast.13, bf16[160,128,128]{2,1,0:T(8,128)(2,1)} %gather_fusion.1, pred[160]{0:T(512)(128)(4,1)S(1)} %compare_and_fusion), kind=kOutput, calls=%fused_computation.6 | convolution fusion | flops 1347420160 | bytes 26214560 | tf_op jit(solution)/shard_map/nik,nlk->nil/dot_general | solution.py:20
  331.0 4.8 reduce_sum.59
  335.8 252.4 %all-reduce.8 = bf16[10,128,128]{2,1,0:T(8,128)(2,1)} all-reduce(f32[10,128,128]{2,1,0:T(8,128)S(1)} %reduce_sum.59), channel_id=1, replica_groups=mesh['op'=64,'sec'=4] {'op'}, use_global_device_ids=true, to_apply=%region_11.13 | all-reduce | flops 163840 | bytes 983040 | tf_op jit(solution)/shard_map/psum | solution.py:42
  (3 shorter events, 0.0 us)
Async XLA Ops:
  7.2 32.8 %all-gather.3.cloned.1.call-start = ((), (), s32[]{:S(2)}) async-start(), calls=%async_computation | async-start | bytes 1638400 | tf_op jit(solution)/shard_map/all_gather | solution.py:8
  7.9 244.4 %all-reduce.7.cloned.1.call-start = ((), (), s32[]{:S(2)}) async-start(), calls=%async_computation.1 | async-start | bytes 1310720 | tf_op jit(solution)/shard_map/psum | solution.py:42
  63.8 188.5 %copy-start = (bf16[10,128,128]{2,1,0:T(8,128)(2,1)S(1)}, bf16[10,128,128]{2,1,0:T(8,128)(2,1)}, u32[]{:S(2)}) copy-start(bf16[10,128,128]{2,1,0:T(8,128)(2,1)} %param.7) | copy-start | bytes 983044
  63.8 200.8 %copy-start.1 = (f32[10,128,128]{2,1,0:T(8,128)S(1)}, f32[10,128,128]{2,1,0:T(8,128)}, u32[]{:S(2)}) copy-start(f32[10,128,128]{2,1,0:T(8,128)} %param.8) | copy-start | bytes 1966084
  69.6 237.5 %all-gather.5.cloned.1.call-start = ((), (), s32[]{:S(2)}) async-start(), calls=%async_computation.2 | async-start | bytes 1638400 | tf_op jit(solution)/shard_map/all_gather | solution.py:8
Sparse Core Ops, SparseCore 0:
  9.8 30.0 all-gather.2
  69.7 182.5 all-reduce.6
  279.4 27.6 all-gather.4
where the time goes:
time: 599 us; the launch traced here: 595 us
  blocking collectives  268 us (45%)
  waiting for transfers between devices  242 us (40%)
  matrix products  29.6 us (5%)
  between operations  19.2 us (3%)
  local copies, waits for them, and re-layouts  19 us (3%)
  other arithmetic  16.2 us (3%)
    psum x1, blocking collectives, whole_sum(): return lax.psum(summands, 'op')  252 us
    psum x1, waiting for transfers between devices, whole_sum(): return lax.psum(summands, 'op')  183 us
    all_gather x2, waiting for transfers between devices, build_terms(): gathered = lax.all_gather(vector, 'sec', axis=0, tiled=True)  59 us
    dot_general x2, matrix products, build_terms(): jnp.einsum('nik,nlk->nil', halfway, right_flat, preferred_element_type=jn...  29.6 us
    gather x2, local copies, waits for them, and re-layouts, build_terms(): sources = jnp.take(padded, connect.reshape(-1), axis=0)  15.3 us
  transfers between devices with their start and end apart: 3, of which 3 were waited for; matrix products, arithmetic and copies ran while one was open for 0% of the time, Pallas kernels for 0%

commit v1 on v0

v1 whole, which is shorter than its diff:
```python
import functools

import jax
import jax.numpy as jnp
from jax import lax
from jax.experimental import pallas as pl
from jax.experimental.pallas import tpu as pltpu
from jax.sharding import PartitionSpec as P

MESH = pl.DeviceIdType.MESH
BS = 128
NZ, NX, NC, NY = 8, 4, 2, 4
PLANE = NZ * NX * NC
SECD = 10
HALF = SECD // NC
PIECE = BS // NX
NSEC = SECD * NY
PAIRD = 16
NT = (((1,), (1,)), ((), ()))
FAR_Z = (4, 3, 5, 2, 6, 1, 7)
FAR_Y = (2, 1, 3)
FAR_X = (2, 1, 3)
LOADS = 4


def sum_z(k):
    return (NZ * k) // HALF


def kernel(
    psi_hbm, diag_hbm, left_hbm, right_hbm, link,
    one_out, corr_out, two_out,
    left, right, vec, diag, sig, raw, corr, part, inbox, two,
    load_sem, out_sem, vsend, vrecv, vfsend, vfrecv, dsend, drecv, dfsend, dfrecv,
    rs_send, rs_recv, z_send, z_recv, xy_send, xy_recv, sib_send, sib_recv,
    x_send, x_recv, sib2_send, sib2_recv,
):
    op = lax.axis_index("op")
    y = lax.axis_index("sec")
    z, x, c = op // (NX * NC), (op // NC) % NX, op % NC

    def at(z_, x_, c_, y_):
        return ((z_ * NX + x_) * NC + c_, y_)

    sibling = at(z, x, 1 - c, y)

    def remote(src, dst, send, recv, device):
        return pltpu.make_async_remote_copy(
            src_ref=src, dst_ref=dst, send_sem=send, recv_sem=recv, device_id=device, device_id_type=MESH
        )

    def settle(ref, sem):
        pltpu.make_async_copy(ref, ref, sem).wait()

    per = PAIRD // LOADS
    loads = []
    for n in range(LOADS):
        rows = pl.ds(n * per, per)
        loads.append(pltpu.make_async_copy(left_hbm.at[rows], left.at[rows], load_sem.at[2 * n]))
        loads.append(pltpu.make_async_copy(right_hbm.at[rows], right.at[rows], load_sem.at[2 * n + 1]))
    own_vec = pltpu.make_async_copy(psi_hbm, vec.at[pl.ds(y * SECD, SECD)], load_sem.at[2 * LOADS])
    own_diag = pltpu.make_async_copy(diag_hbm, diag.at[pl.ds(y * SECD, SECD)], load_sem.at[2 * LOADS + 1])
    own_vec.start()
    for load in loads:
        load.start()
    own_diag.start()

    barrier = pltpu.get_barrier_semaphore()

    def greet(i, _):
        pl.semaphore_signal(barrier, inc=1, device_id=((op + i) % PLANE, y), device_id_type=MESH)
        return 0

    for dy in FAR_Y:
        for dx in range(NX):
            pl.semaphore_signal(
                barrier, inc=1, device_id=at(z, (x + dx) % NX, c, (y + dy) % NY), device_id_type=MESH
            )
    lax.fori_loop(1, PLANE, greet, 0)
    vec[NSEC] = jnp.zeros((BS, BS), jnp.bfloat16)
    corr[NSEC] = jnp.zeros((BS, BS), jnp.bfloat16)
    pl.semaphore_wait(barrier, PLANE - 1 + (NY - 1) * NX)

    for dy in FAR_Y:
        there = at(z, x, c, (y + dy) % NY)
        remote(
            psi_hbm.at[pl.ds(c * HALF, HALF)], vec.at[pl.ds(y * SECD + c * HALF, HALF)],
            vsend, vrecv.at[dy], there,
        ).start()
    own_vec.wait()
    for dy in (1, 3, 2):
        rows = pl.ds(((y + NY - dy) % NY) * SECD + c * HALF, HALF)
        settle(vec.at[rows], vrecv.at[dy])
        remote(vec.at[rows], vec.at[rows], vfsend, vfrecv.at[dy], sibling).start()
    for dy in FAR_Y:
        there = at(z, x, c, (y + dy) % NY)
        remote(
            diag_hbm.at[pl.ds(c * HALF, HALF)], diag.at[pl.ds(y * SECD + c * HALF, HALF)],
            dsend, drecv.at[dy], there,
        ).start()
    for load in loads:
        load.wait()
    for dy in (1, 3, 2):
        rows = pl.ds(((y + NY - dy) % NY) * SECD + (1 - c) * HALF, HALF)
        settle(vec.at[rows], vfrecv.at[dy])

    k_me = (HALF * z + HALF + 2) // NZ
    summing = sum_z(k_me) == z
    mine = pl.ds(x * PIECE, PIECE)

    def apply(which, vector):
        def sector(i, _):
            core, k = i % NC, i // NC
            b = core * HALF + k
            halves = []
            for p in range(PAIRD):
                half = jnp.dot(left[p, b], vector[link[p, b]], preferred_element_type=jnp.float32)
                halves.append(half.astype(jnp.bfloat16))
            halfway = jnp.concatenate(halves, axis=1)
            wide = jnp.concatenate([right[p, b] for p in range(PAIRD)], axis=1)
            total = lax.dot_general(halfway, wide, NT, preferred_element_type=jnp.float32)
            part[which, b] = total.astype(jnp.bfloat16)

            def piece(j, _):
                rows = pl.ds(j * PIECE, PIECE)
                owner = (sum_z(k) * NX + j) * NC + core

                @pl.when(owner == op)
                def _():
                    inbox[which, op] = part[which, b, rows]

                @pl.when(owner != op)
                def _():
                    remote(
                        part.at[which, b, rows], inbox.at[which, op],
                        rs_send.at[which], rs_recv.at[which], (owner, y),
                    ).start()

                return 0

            lax.fori_loop(0, NX, piece, 0)
            return 0

        lax.fori_loop(0, SECD, sector, 0)

    def summed(which):
        settle(inbox.at[which, pl.ds(0, PLANE - 1)], rs_recv.at[which])
        return jnp.sum(inbox[which].astype(jnp.float32), axis=0).astype(jnp.bfloat16)

    apply(0, vec)

    @pl.when(summing)
    def _():
        spot = sig.at[y, c * HALF + k_me, mine]
        spot[...] = summed(0)
        for dz in FAR_Z:
            remote(spot, spot, z_send.at[0], z_recv.at[0, k_me], at((z + dz) % NZ, x, c, y)).start()

    def spread(k, _):
        spot = sig.at[y, c * HALF + k, mine]

        @pl.when(sum_z(k) != z)
        def _():
            settle(spot, z_recv.at[0, k])

        for dy in (2, 1, 3, 0):
            for dx in (2, 1, 3, 0):
                if dx or dy:
                    there = at(z, (x + dx) % NX, c, (y + dy) % NY)
                    remote(spot, spot, xy_send.at[k], xy_recv.at[k], there).start()
        return 0

    lax.fori_loop(0, HALF, spread, 0)
    for dy in (1, 3, 2):
        rows = pl.ds(((y + NY - dy) % NY) * SECD + c * HALF, HALF)
        settle(diag.at[rows], drecv.at[dy])
        remote(diag.at[rows], diag.at[rows], dfsend, dfrecv.at[dy], sibling).start()

    def hand(k, _):
        settle(inbox.at[0, pl.ds(0, NX * NY - 1)], xy_recv.at[k])
        spot = sig.at[:, c * HALF + k]
        remote(spot, spot, sib_send, sib_recv.at[k], sibling).start()
        return 0

    lax.fori_loop(0, HALF, hand, 0)
    own_diag.wait()
    for dy in (1, 3, 2):
        rows = pl.ds(((y + NY - dy) % NY) * SECD + (1 - c) * HALF, HALF)
        settle(diag.at[rows], dfrecv.at[dy])
    for k in range(HALF):
        settle(sig.at[:, (1 - c) * HALF + k], sib_recv.at[k])
    one_copy = pltpu.make_async_copy(sig.at[y], one_out, out_sem.at[0])
    one_copy.start()

    def fold(block):
        return jnp.sum(block.reshape(BS // 8, 8, BS), axis=0)

    def first(s, sums):
        psi = vec[s].astype(jnp.float32)
        sigma = sig[s // SECD, s % SECD].astype(jnp.float32)
        return sums[0] + fold(psi * sigma), sums[1] + fold(psi * psi)

    zero = jnp.zeros((8, BS), jnp.float32)
    correlation, weight = lax.fori_loop(0, NSEC, first, (zero, zero))
    correlation = jnp.sum(correlation, keepdims=True)
    weight = jnp.sum(weight, keepdims=True)
    rayleigh = correlation / weight

    def second(s, sums):
        psi = vec[s].astype(jnp.float32)
        sigma = sig[s // SECD, s % SECD].astype(jnp.float32)
        shifted = diag[s] - rayleigh
        unscaled = (sigma - rayleigh * psi) * shifted / (shifted * shifted + 1.0)
        raw[s] = unscaled
        return sums[0] + fold(psi * unscaled), sums[1] + fold(unscaled * unscaled)

    along, squares = lax.fori_loop(0, NSEC, second, (zero, zero))
    along = jnp.sum(along, keepdims=True)
    squares = jnp.sum(squares, keepdims=True)
    rescale = 1.0 / jnp.sqrt((squares - along * along / weight) / float(NSEC * BS * BS) + 1e-06)
    share = along / weight

    def third(s, _):
        psi = vec[s].astype(jnp.float32)
        corr[s] = ((raw[s] - share * psi) * rescale).astype(jnp.bfloat16)
        return 0

    lax.fori_loop(0, NSEC, third, 0)
    corr_copy = pltpu.make_async_copy(corr.at[pl.ds(y * SECD, SECD)], corr_out, out_sem.at[1])
    corr_copy.start()

    apply(1, corr)

    @pl.when(summing)
    def _():
        spot = two.at[c * HALF + k_me, mine]
        spot[...] = summed(1)
        for dz in FAR_Z:
            remote(spot, spot, z_send.at[1], z_recv.at[1, k_me], at((z + dz) % NZ, x, c, y)).start()

    def spread_two(k, _):
        spot = two.at[c * HALF + k, mine]

        @pl.when(sum_z(k) != z)
        def _():
            settle(spot, z_recv.at[1, k])

        for dx in FAR_X:
            remote(spot, spot, x_send, x_recv.at[k], at(z, (x + dx) % NX, c, y)).start()
        return 0

    lax.fori_loop(0, HALF, spread_two, 0)

    def hand_two(k, _):
        settle(inbox.at[1, pl.ds(0, NX - 1)], x_recv.at[k])
        spot = two.at[c * HALF + k]
        remote(spot, spot, sib2_send, sib2_recv.at[k], sibling).start()
        return 0

    lax.fori_loop(0, HALF, hand_two, 0)
    for k in range(HALF):
        settle(two.at[(1 - c) * HALF + k], sib2_recv.at[k])
    two_copy = pltpu.make_async_copy(two, two_out, out_sem.at[2])
    two_copy.start()

    settle(vec.at[pl.ds(0, (NY - 1) * HALF)], vsend)
    settle(vec.at[pl.ds(0, (NY - 1) * HALF)], vfsend)
    settle(diag.at[pl.ds(0, (NY - 1) * HALF)], dsend)
    settle(diag.at[pl.ds(0, (NY - 1) * HALF)], dfsend)
    for which in range(2):

        @pl.when(summing)
        def _():
            settle(inbox.at[which, pl.ds(0, SECD * NX - 1)], rs_send.at[which])
            settle(inbox.at[which, pl.ds(0, NZ - 1)], z_send.at[which])

        @pl.when(jnp.logical_not(summing))
        def _():
            settle(inbox.at[which, pl.ds(0, SECD * NX)], rs_send.at[which])

    for k in range(HALF):
        settle(inbox.at[0, pl.ds(0, NX * NY - 1)], xy_send.at[k])
    settle(vec.at[pl.ds(0, NY * HALF)], sib_send)
    settle(inbox.at[0, pl.ds(0, HALF * (NX - 1))], x_send)
    settle(vec.at[pl.ds(0, HALF)], sib2_send)
    one_copy.wait()
    corr_copy.wait()
    two_copy.wait()


def per_device(wavefunction, diagonal, left_ops, right_ops, connect):
    blocks = jax.ShapeDtypeStruct((SECD, BS, BS), jnp.bfloat16)
    dma = pltpu.SemaphoreType.DMA
    hbm = pl.BlockSpec(memory_space=pl.ANY)
    return pl.pallas_call(
        kernel,
        out_shape=(blocks, blocks, blocks),
        in_specs=[hbm, hbm, hbm, hbm, pl.BlockSpec(memory_space=pltpu.SMEM)],
        out_specs=(hbm, hbm, hbm),
        scratch_shapes=[
            pltpu.VMEM((PAIRD, SECD, BS, BS), jnp.bfloat16),
            pltpu.VMEM((PAIRD, SECD, BS, BS), jnp.bfloat16),
            pltpu.VMEM((NSEC + 1, BS, BS), jnp.bfloat16),
            pltpu.VMEM((NSEC, BS, BS), jnp.float32),
            pltpu.VMEM((NY, SECD, BS, BS), jnp.bfloat16),
            pltpu.VMEM((NSEC, BS, BS), jnp.float32),
            pltpu.VMEM((NSEC + 1, BS, BS), jnp.bfloat16),
            pltpu.VMEM((2, SECD, BS, BS), jnp.bfloat16),
            pltpu.VMEM((2, PLANE, PIECE, BS), jnp.bfloat16),
            pltpu.VMEM((SECD, BS, BS), jnp.bfloat16),
            dma((2 * LOADS + 2,)), dma((3,)),
            dma, dma((NY,)), dma, dma((NY,)), dma, dma((NY,)), dma, dma((NY,)),
            dma((2,)), dma((2,)), dma((2,)), dma((2, HALF)),
            dma((HALF,)), dma((HALF,)), dma, dma((HALF,)),
            dma, dma((HALF,)), dma, dma((HALF,)),
        ],
        compiler_params=pltpu.CompilerParams(
            collective_id=0, has_side_effects=True, vmem_limit_bytes=40 * 2**20
        ),
        name="davidson",
    )(wavefunction, diagonal, left_ops, right_ops, connect)


def solution(mesh):
    blocks = P("sec", None, None)
    ops = P("op", "sec", None, None)
    return jax.shard_map(
        per_device,
        mesh=mesh,
        in_specs=(blocks, blocks, ops, ops, P("op", "sec")),
        out_specs=(blocks, blocks, blocks),
        check_vma=False,
    )
```

time: 599 us -> 95.4 us (0.16)
  blocking collectives: 268 us -> 0 us
  waiting for transfers between devices: 242 us -> 0 us
  Pallas kernels: 0 us -> 84.6 us
  matrix products: 29.6 us -> 0 us
  between operations: 19.2 us -> 0.65 us
  other arithmetic: 16.2 us -> 0 us
  local copies, waits for them, and re-layouts: 19 us -> 9.89 us
    psum x3 -> x0, blocking collectives: 268 us -> none  [the longest x1 252 us: whole_sum(): return lax.psum(summands, 'op')]
    psum x1 -> x0, waiting for transfers between devices: 183 us -> none  [whole_sum(): return lax.psum(summands, 'op')]
    pallas_call x0 -> x1, Pallas kernels: none -> 84.6 us  [per_device(): pl.pallas_call(kernel, out_shape=(blocks, blocks, blocks), in_specs=[hbm,...]
    all_gather x2 -> x0, waiting for transfers between devices: 59 us -> none  [build_terms(): gathered = lax.all_gather(vector, 'sec', axis=0, tiled=True)]
    dot_general x2 -> x0, matrix products: 29.6 us -> none  [build_terms(): jnp.einsum('nik,nlk->nil', halfway, right_flat, preferred_element_type=jn...]
    gather x2 -> x0, local copies, waits for them, and re-layouts: 15.3 us -> none  [build_terms(): sources = jnp.take(padded, connect.reshape(-1), axis=0)]
    reduce_sum x4 -> x0, other arithmetic: 15.3 us -> none  [the longest x2 10.5 us: build_terms(): jnp.sum(products.reshape(pair_dev, sec_dev, block_len, block_len), axis=0)]
    unnamed x4 -> x13, local copies, waits for them, and re-layouts: 0.01 us -> 9.89 us
  transfers between devices with their start and end apart: 3 -> 0, of which waited for: 3 -> 0; matrix products, arithmetic and copies ran while one was open for 0% -> 0% of each run, Pallas kernels for 0% -> 0%
where the time goes in v1:
time: 95.4 us; the launch traced here: 95.1 us
  Pallas kernels  84.6 us (89%)
  local copies, waits for them, and re-layouts  9.89 us (10%)
    pallas_call x1, Pallas kernels, per_device(): pl.pallas_call(kernel, out_shape=(blocks, blocks, blocks), in_specs=[hbm,...  84.6 us
    unnamed x13, local copies, waits for them, and re-layouts  9.89 us

profile of v1, /device:TPU:1, one launch (start us, length us, event | category | flops | bytes accessed | tf_op | source)
XLA Modules:
  0.0 95.1 jit_solution(16025232350563592204)
XLA Ops:
  0.6 0.0 copy-start
  0.6 2.5 %copy-done = bf16[16,10,128,128]{3,2,1,0:T(8,128)(2,1)S(1)} copy-done((bf16[16,10,128,128]{3,2,1,0:T(8,128)(2,1)S(1)}, bf16[16,10,128,128]{3,2,1,0:T(8,128)(2,1)}, u32[]{:S(2)}) %copy-start) | copy-done | bytes 5242904
  3.1 0.0 copy-start.1
  3.1 2.5 %copy-done.1 = bf16[16,10,128,128]{3,2,1,0:T(8,128)(2,1)S(1)} copy-done((bf16[16,10,128,128]{3,2,1,0:T(8,128)(2,1)S(1)}, bf16[16,10,128,128]{3,2,1,0:T(8,128)(2,1)}, u32[]{:S(2)}) %copy-start.1) | copy-done | bytes 5242904
  5.6 0.0 copy-start.2
  5.6 1.1 %copy-done.2 = f32[10,128,128]{2,1,0:T(8,128)S(1)} copy-done((f32[10,128,128]{2,1,0:T(8,128)S(1)}, f32[10,128,128]{2,1,0:T(8,128)}, u32[]{:S(2)}) %copy-start.2) | copy-done | bytes 655384
  6.7 0.0 copy-start.3
  6.7 1.0 %copy-done.3 = bf16[10,128,128]{2,1,0:T(8,128)(2,1)S(1)} copy-done((bf16[10,128,128]{2,1,0:T(8,128)(2,1)S(1)}, bf16[10,128,128]{2,1,0:T(8,128)(2,1)}, u32[]{:S(2)}) %copy-start.3) | copy-done | bytes 327704
  7.7 0.0 copy-start.4
  7.7 0.7 copy-done.4
  8.4 84.6 %davidson.1 = (bf16[10,128,128]{2,1,0:T(8,128)(2,1)S(1)}, bf16[10,128,128]{2,1,0:T(8,128)(2,1)S(1)}, bf16[10,128,128]{2,1,0:T(8,128)(2,1)S(1)}) custom-call(bf16[10,128,128]{2,1,0:T(8,128)(2,1)S(1)} %copy-done.3, f32[10,128,128]{2,1,0:T(8,128)S(1)} %copy-done.2, bf16[16,10,128,128]{3,2,1,0:T(8,128)(2,1)S(1)} %copy-done, ...), custom_call_target="tpu_custom_call" | custom-call | tf_op jit(solution)/shard_map/davidson/pallas_call | solution.py:295
  92.9 0.7 copy.11
  93.7 0.7 copy.12
  94.4 0.7 copy.13
Async XLA Ops:
  0.6 2.5 %copy-start = (bf16[16,10,128,128]{3,2,1,0:T(8,128)(2,1)S(1)}, bf16[16,10,128,128]{3,2,1,0:T(8,128)(2,1)}, u32[]{:S(2)}) copy-start(bf16[16,10,128,128]{3,2,1,0:T(8,128)(2,1)} %left_hbm.1) | copy-start | bytes 15728644
  3.1 2.5 %copy-start.1 = (bf16[16,10,128,128]{3,2,1,0:T(8,128)(2,1)S(1)}, bf16[16,10,128,128]{3,2,1,0:T(8,128)(2,1)}, u32[]{:S(2)}) copy-start(bf16[16,10,128,128]{3,2,1,0:T(8,128)(2,1)} %right_hbm.1) | copy-start | bytes 15728644
  5.6 1.1 %copy-start.2 = (f32[10,128,128]{2,1,0:T(8,128)S(1)}, f32[10,128,128]{2,1,0:T(8,128)}, u32[]{:S(2)}) copy-start(f32[10,128,128]{2,1,0:T(8,128)} %diag_hbm.1) | copy-start | bytes 1966084
  6.7 1.0 %copy-start.3 = (bf16[10,128,128]{2,1,0:T(8,128)(2,1)S(1)}, bf16[10,128,128]{2,1,0:T(8,128)(2,1)}, u32[]{:S(2)}) copy-start(bf16[10,128,128]{2,1,0:T(8,128)(2,1)} %psi_hbm.1) | copy-start | bytes 983044
  7.7 0.7 copy-start.4

commit v2 on v1

v2 whole, which is shorter than its diff:
```python
import functools

import jax
import jax.numpy as jnp
from jax import lax
from jax.experimental import pallas as pl
from jax.experimental.pallas import tpu as pltpu
from jax.sharding import PartitionSpec as P

MESH = pl.DeviceIdType.MESH
BS = 128
NZ, NX, NC, NY = 8, 4, 2, 4
GROUP = NX * NC
SECD = 10
HALF = SECD // NC
PIECE = BS // NX
NSEC = SECD * NY
PAIRD = 16
NT = (((1,), (1,)), ((), ()))
FAR_Z = (4, 3, 5, 2, 6, 1, 7)
FAR = (2, 1, 3)
LOADS = 4


def reciprocal(q):
    guess = pl.reciprocal(q, approx=True)
    guess = guess * (2.0 - q * guess)
    return guess * (2.0 - q * guess)


def kernel(
    psi_hbm, diag_hbm, left_hbm, right_hbm, link,
    one_out, corr_out, two_out,
    left, right, vec, diag, sig, raw, corr, part, inbox, zbox, two,
    load_sem, out_sem, vsend, vrecv, vfsend, vfrecv, dsend, drecv, dfsend, dfrecv,
    s1_send, s1_recv, z_send, z_recv, xy_send, xy_recv, sib_send, sib_recv,
    x_send, x_recv,
):
    op = lax.axis_index("op")
    y = lax.axis_index("sec")
    z, x, c = op // (NX * NC), (op // NC) % NX, op % NC

    def at(z_, x_, c_, y_):
        return ((z_ * NX + x_) * NC + c_, y_)

    sibling = at(z, x, 1 - c, y)

    def send(src, dst, send_sem, recv_sem, device):
        pltpu.make_async_remote_copy(
            src_ref=src, dst_ref=dst, send_sem=send_sem, recv_sem=recv_sem, device_id=device, device_id_type=MESH
        ).start()

    def settle(ref, sem):
        pltpu.make_async_copy(ref, ref, sem).wait()

    per = PAIRD // LOADS
    loads = []
    for n in range(LOADS):
        rows = pl.ds(n * per, per)
        loads.append(pltpu.make_async_copy(left_hbm.at[rows], left.at[rows], load_sem.at[2 * n]))
        loads.append(pltpu.make_async_copy(right_hbm.at[rows], right.at[rows], load_sem.at[2 * n + 1]))
    own_vec = pltpu.make_async_copy(psi_hbm, vec.at[pl.ds(y * SECD, SECD)], load_sem.at[2 * LOADS])
    own_diag = pltpu.make_async_copy(diag_hbm, diag.at[pl.ds(y * SECD, SECD)], load_sem.at[2 * LOADS + 1])
    own_vec.start()
    for load in loads:
        load.start()
    own_diag.start()

    barrier = pltpu.get_barrier_semaphore()
    friends = [at((z + dz) % NZ, x, c, y) for dz in FAR_Z]
    friends += [at(z, (x + dx) % NX, c, (y + dy) % NY) for dy in FAR for dx in range(NX)]
    friends += [at(z, (x + dx) % NX, core, y) for dx in FAR for core in range(NC)]
    friends.append(sibling)
    for friend in friends:
        pl.semaphore_signal(barrier, inc=1, device_id=friend, device_id_type=MESH)
    vec[NSEC] = jnp.zeros((BS, BS), jnp.bfloat16)
    corr[NSEC] = jnp.zeros((BS, BS), jnp.bfloat16)
    pl.semaphore_wait(barrier, len(friends))

    up, down = at(z, x, c, (y + 1) % NY), at(z, x, c, (y + NY - 1) % NY)

    def spot_of(ref, dy, core, rows):
        return ref.at[pl.ds(((y + dy) % NY) * SECD + core * HALF, HALF), rows]

    halves_of = (pl.ds(0, BS // 2), pl.ds(BS // 2, BS // 2))
    whole = pl.ds(0, BS)

    def gather_start(src, dst, ssem, rsem):
        for n, (there, h) in enumerate(((up, 0), (down, 1), (up, 1), (down, 0))):
            send(
                src.at[pl.ds(c * HALF, HALF), halves_of[h]], spot_of(dst, 0, c, halves_of[h]),
                ssem, rsem.at[n], there,
            )

    def gather_forward(dst, ssem, rsem):
        for dy, there, h, n in ((NY - 1, up, 0, 0), (1, down, 1, 1)):
            spot = spot_of(dst, dy, c, halves_of[h])
            settle(spot, rsem.at[n])
            send(spot, spot, ssem, rsem.at[4 + n], there)

    def gather_share(dst, rsem, fssem, frsem):
        for dy, waits in ((NY - 1, (2,)), (1, (3,)), (2, (4, 5))):
            for n in waits:
                settle(spot_of(dst, dy, c, halves_of[0]), rsem.at[n])
            spot = spot_of(dst, dy, c, whole)
            send(spot, spot, fssem, frsem.at[dy], sibling)

    def gather_end(dst, frsem):
        for dy in (NY - 1, 1, 2):
            settle(spot_of(dst, dy, 1 - c, whole), frsem.at[dy])

    gather_start(psi_hbm, vec, vsend, vrecv)
    own_vec.wait()
    gather_forward(vec, vsend, vrecv)
    gather_share(vec, vrecv, vfsend, vfrecv)
    gather_start(diag_hbm, diag, dsend, drecv)
    for load in loads:
        load.wait()
    gather_end(vec, vfrecv)

    mine = pl.ds(x * PIECE, PIECE)

    def apply(which, vector):
        def sector(i, _):
            core, k = i % NC, i // NC
            b = core * HALF + k
            halves = []
            for p in range(PAIRD):
                half = jnp.dot(left[p, b], vector[link[p, b]], preferred_element_type=jnp.float32)
                halves.append(half.astype(jnp.bfloat16))
            halfway = jnp.concatenate(halves, axis=1)
            wide = jnp.concatenate([right[p, b] for p in range(PAIRD)], axis=1)
            total = lax.dot_general(halfway, wide, NT, preferred_element_type=jnp.float32)
            part[which, b] = total.astype(jnp.bfloat16)

            def piece(j, _):
                rows = pl.ds(j * PIECE, PIECE)
                own = jnp.logical_and(core == c, j == x)

                @pl.when(own)
                def _():
                    inbox[which, k, x * NC + c] = part[which, b, rows]

                @pl.when(jnp.logical_not(own))
                def _():
                    send(
                        part.at[which, b, rows], inbox.at[which, k, x * NC + c],
                        s1_send.at[which], s1_recv.at[which, k], at(z, j, core, y),
                    )

                return 0

            lax.fori_loop(0, NX, piece, 0)
            return 0

        lax.fori_loop(0, SECD, sector, 0)

    def added(box, which, k, count):
        total = box[which, k, 0].astype(jnp.float32)
        for n in range(1, count):
            total = total + box[which, k, n].astype(jnp.float32)
        return total.astype(jnp.bfloat16)

    def sum_near(which):
        def step(k, _):
            settle(inbox.at[which, k, pl.ds(0, GROUP - 1)], s1_recv.at[which, k])
            zbox[which, k, z] = added(inbox, which, k, GROUP)
            spot = zbox.at[which, k, z]
            for dz in FAR_Z:
                send(spot, spot, z_send.at[which], z_recv.at[which, k], at((z + dz) % NZ, x, c, y))
            return 0

        lax.fori_loop(0, HALF, step, 0)

    def sum_far(which, k):
        settle(zbox.at[which, k, pl.ds(0, NZ - 1)], z_recv.at[which, k])
        return added(zbox, which, k, NZ)

    apply(0, vec)
    gather_forward(diag, dsend, drecv)
    sum_near(0)
    gather_share(diag, drecv, dfsend, dfrecv)

    def spread(k, _):
        spot = sig.at[y, c * HALF + k, mine]
        spot[...] = sum_far(0, k)
        for dy in (2, 1, 3, 0):
            for dx in (2, 1, 3, 0):
                if dx or dy:
                    there = at(z, (x + dx) % NX, c, (y + dy) % NY)
                    send(spot, spot, xy_send.at[k], xy_recv.at[k], there)
        return 0

    lax.fori_loop(0, HALF, spread, 0)

    def fold(block):
        return jnp.sum(block.reshape(BS // 8, 8, BS), axis=0)

    def first(core, k, sums):
        for g in range(NY):
            psi = vec[g * SECD + core * HALF + k].astype(jnp.float32)
            sigma = sig[g, core * HALF + k].astype(jnp.float32)
            sums = sums[0] + fold(psi * sigma), sums[1] + fold(psi * psi)
        return sums

    def hand(k, sums):
        settle(inbox.at[0, pl.ds(0, 3), pl.ds(0, NX * NY // 3)], xy_recv.at[k])
        spot = sig.at[:, c * HALF + k]
        send(spot, spot, sib_send, sib_recv.at[k], sibling)
        return first(c, k, sums)

    def handed(k, sums):
        settle(sig.at[:, (1 - c) * HALF + k], sib_recv.at[k])
        return first(1 - c, k, sums)

    zero = jnp.zeros((8, BS), jnp.float32)
    sums = lax.fori_loop(0, HALF, hand, (zero, zero))
    correlation, weight = lax.fori_loop(0, HALF, handed, sums)
    one_copy = pltpu.make_async_copy(sig.at[y], one_out, out_sem.at[0])
    one_copy.start()
    own_diag.wait()
    gather_end(diag, dfrecv)

    correlation = jnp.sum(correlation, keepdims=True)
    weight = jnp.sum(weight, keepdims=True)
    rayleigh = correlation / weight

    def second(s, sums):
        psi = vec[s].astype(jnp.float32)
        sigma = sig[s // SECD, s % SECD].astype(jnp.float32)
        shifted = diag[s] - rayleigh
        unscaled = (sigma - rayleigh * psi) * shifted * reciprocal(shifted * shifted + 1.0)
        raw[s] = unscaled
        return sums[0] + fold(psi * unscaled), sums[1] + fold(unscaled * unscaled)

    along, squares = lax.fori_loop(0, NSEC, second, (zero, zero), unroll=2)
    along = jnp.sum(along, keepdims=True)
    squares = jnp.sum(squares, keepdims=True)
    rescale = 1.0 / jnp.sqrt((squares - along * along / weight) / float(NSEC * BS * BS) + 1e-06)
    share = along / weight

    def third(s, _):
        psi = vec[s].astype(jnp.float32)
        corr[s] = ((raw[s] - share * psi) * rescale).astype(jnp.bfloat16)
        return 0

    lax.fori_loop(0, NSEC, third, 0, unroll=2)
    corr_copy = pltpu.make_async_copy(corr.at[pl.ds(y * SECD, SECD)], corr_out, out_sem.at[1])
    corr_copy.start()

    apply(1, corr)
    sum_near(1)

    def spread_two(k, _):
        spot = two.at[c * HALF + k, mine]
        spot[...] = sum_far(1, k)
        for dx in FAR:
            for core in range(NC):
                send(spot, spot, x_send, x_recv.at[k], at(z, (x + dx) % NX, core, y))
        send(spot, spot, x_send, x_recv.at[k], sibling)
        return 0

    lax.fori_loop(0, HALF, spread_two, 0)
    for k in range(HALF):
        settle(inbox.at[1, 0, pl.ds(0, GROUP - 1)], x_recv.at[k])
    two_copy = pltpu.make_async_copy(two, two_out, out_sem.at[2])
    two_copy.start()

    for ref, ssem, fssem in ((vec, vsend, vfsend), (diag, dsend, dfsend)):
        settle(ref.at[pl.ds(0, 3 * HALF)], ssem)
        settle(ref.at[pl.ds(0, 3 * HALF)], fssem)
    for which in range(2):
        settle(inbox.at[which, :, pl.ds(0, GROUP - 1)], s1_send.at[which])
        settle(inbox.at[which, :, pl.ds(0, NZ - 1)], z_send.at[which])
    for k in range(HALF):
        settle(inbox.at[0, pl.ds(0, 3), pl.ds(0, NX * NY // 3)], xy_send.at[k])
    settle(vec.at[pl.ds(0, NY * HALF)], sib_send)
    settle(inbox.at[1, :, pl.ds(0, GROUP - 1)], x_send)
    one_copy.wait()
    corr_copy.wait()
    two_copy.wait()


def passed_on(a, b, c, a_out, b_out, c_out, sems):
    copies = [
        pltpu.make_async_copy(src, dst, sems.at[n])
        for n, (src, dst) in enumerate(((a, a_out), (b, b_out), (c, c_out)))
    ]
    for copy in copies:
        copy.start()
    for copy in copies:
        copy.wait()


def per_device(wavefunction, diagonal, left_ops, right_ops, connect):
    blocks = jax.ShapeDtypeStruct((SECD, BS, BS), jnp.bfloat16)
    dma = pltpu.SemaphoreType.DMA
    hbm = pl.BlockSpec(memory_space=pl.ANY)
    results = pl.pallas_call(
        kernel,
        out_shape=(blocks, blocks, blocks),
        in_specs=[hbm, hbm, hbm, hbm, pl.BlockSpec(memory_space=pltpu.SMEM)],
        out_specs=(hbm, hbm, hbm),
        scratch_shapes=[
            pltpu.VMEM((PAIRD, SECD, BS, BS), jnp.bfloat16),
            pltpu.VMEM((PAIRD, SECD, BS, BS), jnp.bfloat16),
            pltpu.VMEM((NSEC + 1, BS, BS), jnp.bfloat16),
            pltpu.VMEM((NSEC, BS, BS), jnp.float32),
            pltpu.VMEM((NY, SECD, BS, BS), jnp.bfloat16),
            pltpu.VMEM((NSEC, BS, BS), jnp.float32),
            pltpu.VMEM((NSEC + 1, BS, BS), jnp.bfloat16),
            pltpu.VMEM((2, SECD, BS, BS), jnp.bfloat16),
            pltpu.VMEM((2, HALF, GROUP, PIECE, BS), jnp.bfloat16),
            pltpu.VMEM((2, HALF, NZ, PIECE, BS), jnp.bfloat16),
            pltpu.VMEM((SECD, BS, BS), jnp.bfloat16),
            dma((2 * LOADS + 2,)), dma((3,)),
            dma, dma((6,)), dma, dma((NY,)), dma, dma((6,)), dma, dma((NY,)),
            dma((2,)), dma((2, HALF)), dma((2,)), dma((2, HALF)),
            dma((HALF,)), dma((HALF,)), dma, dma((HALF,)),
            dma, dma((HALF,)),
        ],
        compiler_params=pltpu.CompilerParams(
            collective_id=0, has_side_effects=True, vmem_limit_bytes=60 * 2**20
        ),
        name="davidson",
    )(wavefunction, diagonal, left_ops, right_ops, connect)
    return pl.pallas_call(
        passed_on,
        out_shape=(blocks, blocks, blocks),
        in_specs=[pl.BlockSpec(memory_space=pltpu.VMEM)] * 3,
        out_specs=(hbm, hbm, hbm),
        scratch_shapes=[dma((3,))],
        compiler_params=pltpu.CompilerParams(vmem_limit_bytes=60 * 2**20),
        name="passed_on",
    )(*results)


def solution(mesh):
    blocks = P("sec", None, None)
    ops = P("op", "sec", None, None)
    return jax.shard_map(
        per_device,
        mesh=mesh,
        in_specs=(blocks, blocks, ops, ops, P("op", "sec")),
        out_specs=(blocks, blocks, blocks),
        check_vma=False,
    )
```

time: 95.4 us -> 70.6 us (0.74)
  Pallas kernels: 84.6 us -> 69.8 us
  local copies, waits for them, and re-layouts: 9.89 us -> 0 us
    pallas_call x1, Pallas kernels: 84.6 us -> 67.7 us  [per_device(): pl.pallas_call(kernel, out_shape=(blocks, blocks, blocks), in_specs=[hbm,...]
    unnamed x13 -> x0, local copies, waits for them, and re-layouts: 9.89 us -> none
    pallas_call x0 -> x1, Pallas kernels: none -> 2.14 us  [per_device(): pl.pallas_call(passed_on, out_shape=(blocks, blocks, blocks), in_specs=[p...]
where the time goes in v2:
time: 70.6 us; the launch traced here: 70.5 us
  Pallas kernels  69.8 us (99%)
    pallas_call x1, Pallas kernels, per_device(): pl.pallas_call(kernel, out_shape=(blocks, blocks, blocks), in_specs=[hbm,...  67.7 us
    pallas_call x1, Pallas kernels, per_device(): pl.pallas_call(passed_on, out_shape=(blocks, blocks, blocks), in_specs=[p...  2.14 us

profile of v2, /device:TPU:1, one launch (start us, length us, event | category | flops | bytes accessed | tf_op | source)
XLA Modules:
  0.0 70.5 jit_solution(11635137134616372715)
XLA Ops:
  0.6 67.7 %davidson.1 = (bf16[10,128,128]{2,1,0:T(8,128)(2,1)}, bf16[10,128,128]{2,1,0:T(8,128)(2,1)}, bf16[10,128,128]{2,1,0:T(8,128)(2,1)}) custom-call(bf16[10,128,128]{2,1,0:T(8,128)(2,1)} %psi_hbm.1, f32[10,128,128]{2,1,0:T(8,128)} %diag_hbm.1, bf16[16,10,128,128]{3,2,1,0:T(8,128)(2,1)} %left_hbm.1, bf16[16,10,128,128]{3,2,1,0:T(8,128)(2,1)} %right_hbm.1, ...), custom_call_target="tpu_custom_call" | custom-call | tf_op jit(solution)/shard_map/davidson/pallas_call | solution.py:299
  68.3 2.1 %passed_on.1 = (bf16[10,128,128]{2,1,0:T(8,128)(2,1)}, bf16[10,128,128]{2,1,0:T(8,128)(2,1)}, bf16[10,128,128]{2,1,0:T(8,128)(2,1)}) custom-call(bf16[10,128,128]{2,1,0:T(8,128)(2,1)} %get-tuple-element.6.a, bf16[10,128,128]{2,1,0:T(8,128)(2,1)} %get-tuple-element.7.b, bf16[10,128,128]{2,1,0:T(8,128)(2,1)} %get-tuple-element.8.c), custom_call_target="tpu_custom_call" | custom-call | tf_op jit(solution)/shard_map/passed_on/pallas_call | solution.py:327

commit v3 on v2

--- a/solution.py
+++ b/solution.py
@@ -20,6 +20,7 @@
 FAR_Z = (4, 3, 5, 2, 6, 1, 7)
 FAR = (2, 1, 3)
 LOADS = 4
+UNROLL = 1
 
 
 def reciprocal(q):
@@ -31,10 +32,10 @@
 def kernel(
     psi_hbm, diag_hbm, left_hbm, right_hbm, link,
     one_out, corr_out, two_out,
-    left, right, vec, diag, sig, raw, corr, part, inbox, zbox, two,
+    left, right, vec, diag, sig, raw, corr, part, inbox, zbox, kept, two,
     load_sem, out_sem, vsend, vrecv, vfsend, vfrecv, dsend, drecv, dfsend, dfrecv,
     s1_send, s1_recv, z_send, z_recv, xy_send, xy_recv, sib_send, sib_recv,
-    x_send, x_recv,
+    x_send, x_recv, own_sem,
 ):
     op = lax.axis_index("op")
     y = lax.axis_index("sec")
@@ -67,14 +68,18 @@
     own_diag.start()
 
     barrier = pltpu.get_barrier_semaphore()
-    friends = [at((z + dz) % NZ, x, c, y) for dz in FAR_Z]
-    friends += [at(z, (x + dx) % NX, c, (y + dy) % NY) for dy in FAR for dx in range(NX)]
-    friends += [at(z, (x + dx) % NX, core, y) for dx in FAR for core in range(NC)]
-    friends.append(sibling)
+    zs = [(z + dz) % NZ for dz in range(NZ)]
+    xs = [(x + dx) % NX for dx in range(NX)]
+    ys = [(y + dy) % NY for dy in range(NY)]
+    along_z = [at(zs[dz], x, c, y) for dz in FAR_Z]
+    along_x = [at(z, xs[dx], c, y) for dx in FAR]
+    across_x = [at(z, xs[dx], 1 - c, y) for dx in FAR]
+    along_xy = [at(z, xs[dx], c, ys[dy]) for dy in (2, 1, 3, 0) for dx in (2, 1, 3, 0) if dx or dy]
+    friends = along_z + along_xy + across_x + [sibling]
     for friend in friends:
         pl.semaphore_signal(barrier, inc=1, device_id=friend, device_id_type=MESH)
     vec[NSEC] = jnp.zeros((BS, BS), jnp.bfloat16)
-    corr[NSEC] = jnp.zeros((BS, BS), jnp.bfloat16)
+    raw[NSEC] = jnp.zeros((BS, BS), jnp.bfloat16)
     pl.semaphore_wait(barrier, len(friends))
 
     up, down = at(z, x, c, (y + 1) % NY), at(z, x, c, (y + NY - 1) % NY)
@@ -99,10 +104,9 @@
             send(spot, spot, ssem, rsem.at[4 + n], there)
 
     def gather_share(dst, rsem, fssem, frsem):
-        for dy, waits in ((NY - 1, (2,)), (1, (3,)), (2, (4, 5))):
-            for n in waits:
-                settle(spot_of(dst, dy, c, halves_of[0]), rsem.at[n])
-            spot = spot_of(dst, dy, c, whole)
+        for dy, n, rows in ((NY - 1, 2, whole), (1, 3, whole), (2, 4, halves_of[0]), (2, 5, halves_of[1])):
+            settle(spot_of(dst, dy, c, halves_of[0]), rsem.at[n])
+            spot = spot_of(dst, dy, c, rows)
             send(spot, spot, fssem, frsem.at[dy], sibling)
 
     def gather_end(dst, frsem):
@@ -121,53 +125,43 @@
     mine = pl.ds(x * PIECE, PIECE)
 
     def apply(which, vector):
-        def sector(i, _):
-            core, k = i % NC, i // NC
-            b = core * HALF + k
-            halves = []
-            for p in range(PAIRD):
-                half = jnp.dot(left[p, b], vector[link[p, b]], preferred_element_type=jnp.float32)
-                halves.append(half.astype(jnp.bfloat16))
-            halfway = jnp.concatenate(halves, axis=1)
-            wide = jnp.concatenate([right[p, b] for p in range(PAIRD)], axis=1)
-            total = lax.dot_general(halfway, wide, NT, preferred_element_type=jnp.float32)
-            part[which, b] = total.astype(jnp.bfloat16)
-
-            def piece(j, _):
-                rows = pl.ds(j * PIECE, PIECE)
-                own = jnp.logical_and(core == c, j == x)
-
-                @pl.when(own)
-                def _():
-                    inbox[which, k, x * NC + c] = part[which, b, rows]
-
-                @pl.when(jnp.logical_not(own))
-                def _():
-                    send(
-                        part.at[which, b, rows], inbox.at[which, k, x * NC + c],
-                        s1_send.at[which], s1_recv.at[which, k], at(z, j, core, y),
-                    )
-
-                return 0
-
-            lax.fori_loop(0, NX, piece, 0)
+        def step(k, _):
+            for core in (1 - c, c):
+                b = core * HALF + k
+                halves = []
+                for p in range(PAIRD):
+                    half = jnp.dot(left[p, b], vector[link[p, b]], preferred_element_type=jnp.float32)
+                    halves.append(half.astype(jnp.bfloat16))
+                halfway = jnp.concatenate(halves, axis=1)
+                wide = jnp.concatenate([right[p, b] for p in range(PAIRD)], axis=1)
+                total = lax.dot_general(halfway, wide, NT, preferred_element_type=jnp.float32)
+                part[which, b] = total.astype(jnp.bfloat16)
+                for dx, there in zip((2, 1, 3, 0), (along_x if core is c else across_x) + [sibling]):
+                    rows = pl.ds(xs[dx] * PIECE, PIECE)
+                    if core is c and dx == 0:
+                        inbox[which, k, x * NC + c] = part[which, b, rows]
+                    else:
+                        send(
+                            part.at[which, b, rows], inbox.at[which, k, x * NC + c],
+                            s1_send.at[which], s1_recv.at[which, k], there,
+                        )
             return 0
 
-        lax.fori_loop(0, SECD, sector, 0)
+        lax.fori_loop(0, HALF, step, 0, unroll=UNROLL)
 
     def added(box, which, k, count):
         total = box[which, k, 0].astype(jnp.float32)
         for n in range(1, count):
             total = total + box[which, k, n].astype(jnp.float32)
-        return total.astype(jnp.bfloat16)
+        return total
 
     def sum_near(which):
         def step(k, _):
             settle(inbox.at[which, k, pl.ds(0, GROUP - 1)], s1_recv.at[which, k])
-            zbox[which, k, z] = added(inbox, which, k, GROUP)
+            zbox[which, k, z] = added(inbox, which, k, GROUP).astype(jnp.bfloat16)
             spot = zbox.at[which, k, z]
-            for dz in FAR_Z:
-                send(spot, spot, z_send.at[which], z_recv.at[which, k], at((z + dz) % NZ, x, c, y))
+            for there in along_z:
+                send(spot, spot, z_send.at[which], z_recv.at[which, k], there)
             return 0
 
         lax.fori_loop(0, HALF, step, 0)
@@ -179,19 +173,18 @@
     apply(0, vec)
     gather_forward(diag, dsend, drecv)
     sum_near(0)
-    gather_share(diag, drecv, dfsend, dfrecv)
 
     def spread(k, _):
         spot = sig.at[y, c * HALF + k, mine]
-        spot[...] = sum_far(0, k)
-        for dy in (2, 1, 3, 0):
-            for dx in (2, 1, 3, 0):
-                if dx or dy:
-                    there = at(z, (x + dx) % NX, c, (y + dy) % NY)
-                    send(spot, spot, xy_send.at[k], xy_recv.at[k], there)
+        kept[k] = sum_far(0, k)
+        spot[...] = kept[k].astype(jnp.bfloat16)
+        for there in along_xy:
+            send(spot, spot, xy_send.at[k], xy_recv.at[k], there)
         return 0
 
-    lax.fori_loop(0, HALF, spread, 0)
+    lax.fori_loop(0, 2, spread, 0)
+    gather_share(diag, drecv, dfsend, dfrecv)
+    lax.fori_loop(2, HALF, spread, 0)
 
     def fold(block):
         return jnp.sum(block.reshape(BS // 8, 8, BS), axis=0)
@@ -225,46 +218,46 @@
     weight = jnp.sum(weight, keepdims=True)
     rayleigh = correlation / weight
 
-    def second(s, sums):
+    def unscaled_of(s):
         psi = vec[s].astype(jnp.float32)
         sigma = sig[s // SECD, s % SECD].astype(jnp.float32)
         shifted = diag[s] - rayleigh
-        unscaled = (sigma - rayleigh * psi) * shifted * reciprocal(shifted * shifted + 1.0)
-        raw[s] = unscaled
+        return psi, (sigma - rayleigh * psi) * shifted * reciprocal(shifted * shifted + 1.0)
+
+    def second(s, sums):
+        psi, unscaled = unscaled_of(s)
+        raw[s] = unscaled.astype(jnp.bfloat16)
         return sums[0] + fold(psi * unscaled), sums[1] + fold(unscaled * unscaled)
 
     along, squares = lax.fori_loop(0, NSEC, second, (zero, zero), unroll=2)
+
+    apply(1, raw)
     along = jnp.sum(along, keepdims=True)
     squares = jnp.sum(squares, keepdims=True)
     rescale = 1.0 / jnp.sqrt((squares - along * along / weight) / float(NSEC * BS * BS) + 1e-06)
     share = along / weight
-
-    def third(s, _):
-        psi = vec[s].astype(jnp.float32)
-        corr[s] = ((raw[s] - share * psi) * rescale).astype(jnp.bfloat16)
+    sum_near(1)
+
+    def third(n, _):
+        psi, unscaled = unscaled_of(y * SECD + n)
+        corr[n] = ((unscaled - share * psi) * rescale).astype(jnp.bfloat16)
         return 0
 
-    lax.fori_loop(0, NSEC, third, 0, unroll=2)
-    corr_copy = pltpu.make_async_copy(corr.at[pl.ds(y * SECD, SECD)], corr_out, out_sem.at[1])
+    lax.fori_loop(0, SECD, third, 0, unroll=2)
+    corr_copy = pltpu.make_async_copy(corr, corr_out, out_sem.at[1])
     corr_copy.start()
 
-    apply(1, corr)
-    sum_near(1)
-
     def spread_two(k, _):
-        spot = two.at[c * HALF + k, mine]
-        spot[...] = sum_far(1, k)
-        for dx in FAR:
-            for core in range(NC):
-                send(spot, spot, x_send, x_recv.at[k], at(z, (x + dx) % NX, core, y))
-        send(spot, spot, x_send, x_recv.at[k], sibling)
+        spot, there = two.at[k], two_out.at[c * HALF + k, mine]
+        spot[...] = ((sum_far(1, k) - share * kept[k]) * rescale).astype(jnp.bfloat16)
+        for device in along_x + across_x + [sibling]:
+            send(spot, there, x_send, x_recv.at[k], device)
+        pltpu.make_async_copy(spot, there, own_sem).start()
         return 0
 
     lax.fori_loop(0, HALF, spread_two, 0)
     for k in range(HALF):
         settle(inbox.at[1, 0, pl.ds(0, GROUP - 1)], x_recv.at[k])
-    two_copy = pltpu.make_async_copy(two, two_out, out_sem.at[2])
-    two_copy.start()
 
     for ref, ssem, fssem in ((vec, vsend, vfsend), (diag, dsend, dfsend)):
         settle(ref.at[pl.ds(0, 3 * HALF)], ssem)
@@ -278,18 +271,19 @@
     settle(inbox.at[1, :, pl.ds(0, GROUP - 1)], x_send)
     one_copy.wait()
     corr_copy.wait()
-    two_copy.wait()
-
-
-def passed_on(a, b, c, a_out, b_out, c_out, sems):
-    copies = [
-        pltpu.make_async_copy(src, dst, sems.at[n])
-        for n, (src, dst) in enumerate(((a, a_out), (b, b_out), (c, c_out)))
-    ]
-    for copy in copies:
+    settle(two, own_sem)
+
+
+def passed_on(a, b, c, a_out, b_out, c_out, held, sems):
+    ins = [pltpu.make_async_copy(src, held.at[n], sems.at[0, n]) for n, src in enumerate((a, b, c))]
+    outs = [pltpu.make_async_copy(held.at[n], dst, sems.at[1, n]) for n, dst in enumerate((a_out, b_out, c_out))]
+    for copy in ins:
         copy.start()
-    for copy in copies:
+    for copy, onward in zip(ins, outs):
         copy.wait()
+        onward.start()
+    for onward in outs:
+        onward.wait()
 
 
 def per_device(wavefunction, diagonal, left_ops, right_ops, connect):
@@ -307,17 +301,18 @@
             pltpu.VMEM((NSEC + 1, BS, BS), jnp.bfloat16),
             pltpu.VMEM((NSEC, BS, BS), jnp.float32),
             pltpu.VMEM((NY, SECD, BS, BS), jnp.bfloat16),
-            pltpu.VMEM((NSEC, BS, BS), jnp.float32),
             pltpu.VMEM((NSEC + 1, BS, BS), jnp.bfloat16),
+            pltpu.VMEM((SECD, BS, BS), jnp.bfloat16),
             pltpu.VMEM((2, SECD, BS, BS), jnp.bfloat16),
             pltpu.VMEM((2, HALF, GROUP, PIECE, BS), jnp.bfloat16),
             pltpu.VMEM((2, HALF, NZ, PIECE, BS), jnp.bfloat16),
-            pltpu.VMEM((SECD, BS, BS), jnp.bfloat16),
+            pltpu.VMEM((HALF, PIECE, BS), jnp.float32),
+            pltpu.VMEM((HALF, PIECE, BS), jnp.bfloat16),
             dma((2 * LOADS + 2,)), dma((3,)),
             dma, dma((6,)), dma, dma((NY,)), dma, dma((6,)), dma, dma((NY,)),
             dma((2,)), dma((2, HALF)), dma((2,)), dma((2, HALF)),
             dma((HALF,)), dma((HALF,)), dma, dma((HALF,)),
-            dma, dma((HALF,)),
+            dma, dma((HALF,)), dma,
         ],
         compiler_params=pltpu.CompilerParams(
             collective_id=0, has_side_effects=True, vmem_limit_bytes=60 * 2**20
@@ -327,9 +322,9 @@
     return pl.pallas_call(
         passed_on,
         out_shape=(blocks, blocks, blocks),
-        in_specs=[pl.BlockSpec(memory_space=pltpu.VMEM)] * 3,
+        in_specs=[hbm, hbm, hbm],
         out_specs=(hbm, hbm, hbm),
-        scratch_shapes=[dma((3,))],
+        scratch_shapes=[pltpu.VMEM((3, SECD, BS, BS), jnp.bfloat16), dma((2, 3))],
         compiler_params=pltpu.CompilerParams(vmem_limit_bytes=60 * 2**20),
         name="passed_on",
     )(*results)

time: 70.6 us -> 67.2 us (0.952)
  Pallas kernels: 69.8 us -> 66.4 us
    pallas_call x1, Pallas kernels: 67.7 us -> 64.4 us  [per_device(): pl.pallas_call(kernel, out_shape=(blocks, blocks, blocks), in_specs=[hbm,...]
where the time goes in v3:
time: 67.2 us; the launch traced here: 67 us
  Pallas kernels  66.4 us (99%)
    pallas_call x1, Pallas kernels, per_device(): pl.pallas_call(kernel, out_shape=(blocks, blocks, blocks), in_specs=[hbm,...  64.4 us
    pallas_call x1, Pallas kernels, per_device(): pl.pallas_call(passed_on, out_shape=(blocks, blocks, blocks), in_specs=[h...  1.96 us

profile of v3, /device:TPU:1, one launch (start us, length us, event | category | flops | bytes accessed | tf_op | source)
XLA Modules:
  0.0 67.0 jit_solution(1216064142724908598)
XLA Ops:
  0.6 64.4 %davidson.1 = (bf16[10,128,128]{2,1,0:T(8,128)(2,1)}, bf16[10,128,128]{2,1,0:T(8,128)(2,1)}, bf16[10,128,128]{2,1,0:T(8,128)(2,1)}) custom-call(bf16[10,128,128]{2,1,0:T(8,128)(2,1)} %psi_hbm.1, f32[10,128,128]{2,1,0:T(8,128)} %diag_hbm.1, bf16[16,10,128,128]{3,2,1,0:T(8,128)(2,1)} %left_hbm.1, bf16[16,10,128,128]{3,2,1,0:T(8,128)(2,1)} %right_hbm.1, ...), custom_call_target="tpu_custom_call" | custom-call | tf_op jit(solution)/shard_map/davidson/pallas_call | solution.py:293
  65.1 2.0 %passed_on.1 = (bf16[10,128,128]{2,1,0:T(8,128)(2,1)}, bf16[10,128,128]{2,1,0:T(8,128)(2,1)}, bf16[10,128,128]{2,1,0:T(8,128)(2,1)}) custom-call(bf16[10,128,128]{2,1,0:T(8,128)(2,1)} %get-tuple-element.6.a, bf16[10,128,128]{2,1,0:T(8,128)(2,1)} %get-tuple-element.7.b, bf16[10,128,128]{2,1,0:T(8,128)(2,1)} %get-tuple-element.8.c), custom_call_target="tpu_custom_call" | custom-call | tf_op jit(solution)/shard_map/passed_on/pallas_call | solution.py:322

commit v4 on v3

--- a/solution.py
+++ b/solution.py
@@ -21,6 +21,7 @@
 FAR = (2, 1, 3)
 LOADS = 4
 UNROLL = 1
+CUTS = 2
 
 
 def reciprocal(q):
@@ -54,6 +55,18 @@
     def settle(ref, sem):
         pltpu.make_async_copy(ref, ref, sem).wait()
 
+    barrier = pltpu.get_barrier_semaphore()
+    zs = [(z + dz) % NZ for dz in range(NZ)]
+    xs = [(x + dx) % NX for dx in range(NX)]
+    ys = [(y + dy) % NY for dy in range(NY)]
+    along_z = [at(zs[dz], x, c, y) for dz in FAR_Z]
+    along_x = [at(z, xs[dx], c, y) for dx in FAR]
+    across_x = [at(z, xs[dx], 1 - c, y) for dx in FAR]
+    along_xy = [at(z, xs[dx], c, ys[dy]) for dy in (2, 1, 3, 0) for dx in (2, 1, 3, 0) if dx or dy]
+    friends = [at(z, x, c, ys[dy]) for dy in FAR] + along_z + along_x + across_x + [sibling]
+    friends += [at(z, xs[dx], c, ys[dy]) for dy in FAR for dx in FAR]
+    for friend in friends:
+        pl.semaphore_signal(barrier, inc=1, device_id=friend, device_id_type=MESH)
     per = PAIRD // LOADS
     loads = []
     for n in range(LOADS):
@@ -67,17 +80,6 @@
         load.start()
     own_diag.start()
 
-    barrier = pltpu.get_barrier_semaphore()
-    zs = [(z + dz) % NZ for dz in range(NZ)]
-    xs = [(x + dx) % NX for dx in range(NX)]
-    ys = [(y + dy) % NY for dy in range(NY)]
-    along_z = [at(zs[dz], x, c, y) for dz in FAR_Z]
-    along_x = [at(z, xs[dx], c, y) for dx in FAR]
-    across_x = [at(z, xs[dx], 1 - c, y) for dx in FAR]
-    along_xy = [at(z, xs[dx], c, ys[dy]) for dy in (2, 1, 3, 0) for dx in (2, 1, 3, 0) if dx or dy]
-    friends = along_z + along_xy + across_x + [sibling]
-    for friend in friends:
-        pl.semaphore_signal(barrier, inc=1, device_id=friend, device_id_type=MESH)
     vec[NSEC] = jnp.zeros((BS, BS), jnp.bfloat16)
     raw[NSEC] = jnp.zeros((BS, BS), jnp.bfloat16)
     pl.semaphore_wait(barrier, len(friends))
@@ -87,27 +89,41 @@
     def spot_of(ref, dy, core, rows):
         return ref.at[pl.ds(((y + dy) % NY) * SECD + core * HALF, HALF), rows]
 
-    halves_of = (pl.ds(0, BS // 2), pl.ds(BS // 2, BS // 2))
+    chunks = [pl.ds(q * (BS // CUTS), BS // CUTS) for q in range(CUTS)]
     whole = pl.ds(0, BS)
+    early, late = range(CUTS // 2), range(CUTS // 2, CUTS)
 
     def gather_start(src, dst, ssem, rsem):
-        for n, (there, h) in enumerate(((up, 0), (down, 1), (up, 1), (down, 0))):
-            send(
-                src.at[pl.ds(c * HALF, HALF), halves_of[h]], spot_of(dst, 0, c, halves_of[h]),
-                ssem, rsem.at[n], there,
-            )
+        for q in range(CUTS):
+            for there, h, base in ((up, q, 0), (down, (q + CUTS // 2) % CUTS, CUTS)):
+                send(
+                    src.at[pl.ds(c * HALF, HALF), chunks[h]], spot_of(dst, 0, c, chunks[h]),
+                    ssem, rsem.at[base + h], there,
+                )
 
     def gather_forward(dst, ssem, rsem):
-        for dy, there, h, n in ((NY - 1, up, 0, 0), (1, down, 1, 1)):
-            spot = spot_of(dst, dy, c, halves_of[h])
-            settle(spot, rsem.at[n])
-            send(spot, spot, ssem, rsem.at[4 + n], there)
+        for q in early:
+            for dy, there, h, base in ((NY - 1, up, q, 0), (1, down, q + CUTS // 2, CUTS)):
+                spot = spot_of(dst, dy, c, chunks[h])
+                settle(spot, rsem.at[base + h])
+                send(spot, spot, ssem, rsem.at[2 * CUTS + h], there)
 
     def gather_share(dst, rsem, fssem, frsem):
-        for dy, n, rows in ((NY - 1, 2, whole), (1, 3, whole), (2, 4, halves_of[0]), (2, 5, halves_of[1])):
-            settle(spot_of(dst, dy, c, halves_of[0]), rsem.at[n])
-            spot = spot_of(dst, dy, c, rows)
+        def share(dy, h):
+            spot = spot_of(dst, dy, c, chunks[h])
             send(spot, spot, fssem, frsem.at[dy], sibling)
+
+        for q in early:
+            share(NY - 1, q)
+            share(1, q + CUTS // 2)
+        for q in early:
+            for dy, h, base in ((NY - 1, q + CUTS // 2, 0), (1, q, CUTS)):
+                settle(spot_of(dst, dy, c, chunks[h]), rsem.at[base + h])
+                share(dy, h)
+        for q in early:
+            for h in (q, q + CUTS // 2):
+                settle(spot_of(dst, 2, c, chunks[h]), rsem.at[2 * CUTS + h])
+                share(2, h)
 
     def gather_end(dst, frsem):
         for dy in (NY - 1, 1, 2):
@@ -126,7 +142,7 @@
 
     def apply(which, vector):
         def step(k, _):
-            for core in (1 - c, c):
+            for core in (c, 1 - c):
                 b = core * HALF + k
                 halves = []
                 for p in range(PAIRD):
@@ -147,7 +163,10 @@
                         )
             return 0
 
-        lax.fori_loop(0, HALF, step, 0, unroll=UNROLL)
+        for lo, hi, near in ((0, 4, 0), (4, 5, 1)):
+            lax.fori_loop(lo, hi, step, 0)
+            if near:
+                sum_near(which, 0, near)
 
     def added(box, which, k, count):
         total = box[which, k, 0].astype(jnp.float32)
@@ -155,7 +174,7 @@
             total = total + box[which, k, n].astype(jnp.float32)
         return total
 
-    def sum_near(which):
+    def sum_near(which, lo=0, hi=HALF):
         def step(k, _):
             settle(inbox.at[which, k, pl.ds(0, GROUP - 1)], s1_recv.at[which, k])
             zbox[which, k, z] = added(inbox, which, k, GROUP).astype(jnp.bfloat16)
@@ -164,7 +183,7 @@
                 send(spot, spot, z_send.at[which], z_recv.at[which, k], there)
             return 0
 
-        lax.fori_loop(0, HALF, step, 0)
+        lax.fori_loop(lo, hi, step, 0, unroll=hi - lo)
 
     def sum_far(which, k):
         settle(zbox.at[which, k, pl.ds(0, NZ - 1)], z_recv.at[which, k])
@@ -172,7 +191,7 @@
 
     apply(0, vec)
     gather_forward(diag, dsend, drecv)
-    sum_near(0)
+    sum_near(0, 1)
 
     def spread(k, _):
         spot = sig.at[y, c * HALF + k, mine]
@@ -182,9 +201,9 @@
             send(spot, spot, xy_send.at[k], xy_recv.at[k], there)
         return 0
 
-    lax.fori_loop(0, 2, spread, 0)
+    lax.fori_loop(0, 2, spread, 0, unroll=2)
     gather_share(diag, drecv, dfsend, dfrecv)
-    lax.fori_loop(2, HALF, spread, 0)
+    lax.fori_loop(2, HALF, spread, 0, unroll=HALF - 2)
 
     def fold(block):
         return jnp.sum(block.reshape(BS // 8, 8, BS), axis=0)
@@ -207,8 +226,8 @@
         return first(1 - c, k, sums)
 
     zero = jnp.zeros((8, BS), jnp.float32)
-    sums = lax.fori_loop(0, HALF, hand, (zero, zero))
-    correlation, weight = lax.fori_loop(0, HALF, handed, sums)
+    sums = lax.fori_loop(0, HALF, hand, (zero, zero), unroll=HALF)
+    correlation, weight = lax.fori_loop(0, HALF, handed, sums, unroll=HALF)
     one_copy = pltpu.make_async_copy(sig.at[y], one_out, out_sem.at[0])
     one_copy.start()
     own_diag.wait()
@@ -229,14 +248,14 @@
         raw[s] = unscaled.astype(jnp.bfloat16)
         return sums[0] + fold(psi * unscaled), sums[1] + fold(unscaled * unscaled)
 
-    along, squares = lax.fori_loop(0, NSEC, second, (zero, zero), unroll=2)
+    along, squares = lax.fori_loop(0, NSEC, second, (zero, zero), unroll=4)
 
     apply(1, raw)
     along = jnp.sum(along, keepdims=True)
     squares = jnp.sum(squares, keepdims=True)
     rescale = 1.0 / jnp.sqrt((squares - along * along / weight) / float(NSEC * BS * BS) + 1e-06)
     share = along / weight
-    sum_near(1)
+    sum_near(1, 1)
 
     def third(n, _):
         psi, unscaled = unscaled_of(y * SECD + n)
@@ -255,7 +274,7 @@
         pltpu.make_async_copy(spot, there, own_sem).start()
         return 0
 
-    lax.fori_loop(0, HALF, spread_two, 0)
+    lax.fori_loop(0, HALF, spread_two, 0, unroll=HALF)
     for k in range(HALF):
         settle(inbox.at[1, 0, pl.ds(0, GROUP - 1)], x_recv.at[k])
 
@@ -309,7 +328,7 @@
             pltpu.VMEM((HALF, PIECE, BS), jnp.float32),
             pltpu.VMEM((HALF, PIECE, BS), jnp.bfloat16),
             dma((2 * LOADS + 2,)), dma((3,)),
-            dma, dma((6,)), dma, dma((NY,)), dma, dma((6,)), dma, dma((NY,)),
+            dma, dma((3 * CUTS,)), dma, dma((NY,)), dma, dma((3 * CUTS,)), dma, dma((NY,)),
             dma((2,)), dma((2, HALF)), dma((2,)), dma((2, HALF)),
             dma((HALF,)), dma((HALF,)), dma, dma((HALF,)),
             dma, dma((HALF,)), dma,

time: 67.2 us -> 66.6 us (level)
  no operation moved by 1% of the time
where the time goes in v4:
time: 66.6 us; the launch traced here: 66.4 us
  Pallas kernels  65.8 us (99%)
    pallas_call x1, Pallas kernels, per_device(): pl.pallas_call(kernel, out_shape=(blocks, blocks, blocks), in_specs=[hbm,...  63.8 us
    pallas_call x1, Pallas kernels, per_device(): pl.pallas_call(passed_on, out_shape=(blocks, blocks, blocks), in_specs=[h...  1.96 us

profile of v4, /device:TPU:1, one launch (start us, length us, event | category | flops | bytes accessed | tf_op | source)
XLA Modules:
  0.0 66.4 jit_solution(13190004497152486165)
XLA Ops:
  0.6 63.8 %davidson.1 = (bf16[10,128,128]{2,1,0:T(8,128)(2,1)}, bf16[10,128,128]{2,1,0:T(8,128)(2,1)}, bf16[10,128,128]{2,1,0:T(8,128)(2,1)}) custom-call(bf16[10,128,128]{2,1,0:T(8,128)(2,1)} %psi_hbm.1, f32[10,128,128]{2,1,0:T(8,128)} %diag_hbm.1, bf16[16,10,128,128]{3,2,1,0:T(8,128)(2,1)} %left_hbm.1, bf16[16,10,128,128]{3,2,1,0:T(8,128)(2,1)} %right_hbm.1, ...), custom_call_target="tpu_custom_call" | custom-call | tf_op jit(solution)/shard_map/davidson/pallas_call | solution.py:312
  64.4 2.0 %passed_on.1 = (bf16[10,128,128]{2,1,0:T(8,128)(2,1)}, bf16[10,128,128]{2,1,0:T(8,128)(2,1)}, bf16[10,128,128]{2,1,0:T(8,128)(2,1)}) custom-call(bf16[10,128,128]{2,1,0:T(8,128)(2,1)} %get-tuple-element.6.a, bf16[10,128,128]{2,1,0:T(8,128)(2,1)} %get-tuple-element.7.b, bf16[10,128,128]{2,1,0:T(8,128)(2,1)} %get-tuple-element.8.c), custom_call_target="tpu_custom_call" | custom-call | tf_op jit(solution)/shard_map/passed_on/pallas_call | solution.py:341

commit v5 on v4

--- a/solution.py
+++ b/solution.py
@@ -269,7 +269,7 @@
     def spread_two(k, _):
         spot, there = two.at[k], two_out.at[c * HALF + k, mine]
         spot[...] = ((sum_far(1, k) - share * kept[k]) * rescale).astype(jnp.bfloat16)
-        for device in along_x + across_x + [sibling]:
+        for device in [across_x[0], along_x[0]] + across_x[1:] + along_x[1:] + [sibling]:
             send(spot, there, x_send, x_recv.at[k], device)
         pltpu.make_async_copy(spot, there, own_sem).start()
         return 0
@@ -294,8 +294,12 @@
 
 
 def passed_on(a, b, c, a_out, b_out, c_out, held, sems):
-    ins = [pltpu.make_async_copy(src, held.at[n], sems.at[0, n]) for n, src in enumerate((a, b, c))]
-    outs = [pltpu.make_async_copy(held.at[n], dst, sems.at[1, n]) for n, dst in enumerate((a_out, b_out, c_out))]
+    ins, outs = [], []
+    for n, (src, dst) in enumerate(((a, a_out), (b, b_out), (c, c_out))):
+        for h in range(2):
+            rows = pl.ds(h * HALF, HALF)
+            ins.append(pltpu.make_async_copy(src.at[rows], held.at[n, rows], sems.at[0, 2 * n + h]))
+            outs.append(pltpu.make_async_copy(held.at[n, rows], dst.at[rows], sems.at[1, 2 * n + h]))
     for copy in ins:
         copy.start()
     for copy, onward in zip(ins, outs):
@@ -343,7 +347,7 @@
         out_shape=(blocks, blocks, blocks),
         in_specs=[hbm, hbm, hbm],
         out_specs=(hbm, hbm, hbm),
-        scratch_shapes=[pltpu.VMEM((3, SECD, BS, BS), jnp.bfloat16), dma((2, 3))],
+        scratch_shapes=[pltpu.VMEM((3, SECD, BS, BS), jnp.bfloat16), dma((2, 6))],
         compiler_params=pltpu.CompilerParams(vmem_limit_bytes=60 * 2**20),
         name="passed_on",
     )(*results)

time: 66.6 us -> 66.5 us (level)
  no operation moved by 1% of the time
where the time goes in v5:
time: 66.5 us; the launch traced here: 66.4 us
  Pallas kernels  65.7 us (99%)
    pallas_call x1, Pallas kernels, per_device(): pl.pallas_call(kernel, out_shape=(blocks, blocks, blocks), in_specs=[hbm,...  63.7 us
    pallas_call x1, Pallas kernels, per_device(): pl.pallas_call(passed_on, out_shape=(blocks, blocks, blocks), in_specs=[h...  2.06 us

profile of v5, /device:TPU:1, one launch (start us, length us, event | category | flops | bytes accessed | tf_op | source)
XLA Modules:
  0.0 66.4 jit_solution(4888153012732199500)
XLA Ops:
  0.6 63.7 %davidson.1 = (bf16[10,128,128]{2,1,0:T(8,128)(2,1)}, bf16[10,128,128]{2,1,0:T(8,128)(2,1)}, bf16[10,128,128]{2,1,0:T(8,128)(2,1)}) custom-call(bf16[10,128,128]{2,1,0:T(8,128)(2,1)} %psi_hbm.1, f32[10,128,128]{2,1,0:T(8,128)} %diag_hbm.1, bf16[16,10,128,128]{3,2,1,0:T(8,128)(2,1)} %left_hbm.1, bf16[16,10,128,128]{3,2,1,0:T(8,128)(2,1)} %right_hbm.1, ...), custom_call_target="tpu_custom_call" | custom-call | tf_op jit(solution)/shard_map/davidson/pallas_call | solution.py:316
  64.3 2.1 %passed_on.1 = (bf16[10,128,128]{2,1,0:T(8,128)(2,1)}, bf16[10,128,128]{2,1,0:T(8,128)(2,1)}, bf16[10,128,128]{2,1,0:T(8,128)(2,1)}) custom-call(bf16[10,128,128]{2,1,0:T(8,128)(2,1)} %get-tuple-element.6.a, bf16[10,128,128]{2,1,0:T(8,128)(2,1)} %get-tuple-element.7.b, bf16[10,128,128]{2,1,0:T(8,128)(2,1)} %get-tuple-element.8.c), custom_call_target="tpu_custom_call" | custom-call | tf_op jit(solution)/shard_map/passed_on/pallas_call | solution.py:345
